TPU v7x, 128 devices: a whole 4x4x4 slice. The times are simulated.
128 devices in a mesh: row: 8 (over x, z_lo), col: 16 (over z_hi, y, core).
Axes of the slice: x: 4, y: 4, z: 4 (z_hi: 2, z_lo: 2; z = z_hi * 2 + z_lo), core: 2. Of those that a mesh axis runs over, the one named last changes fastest.
Arguments:
- object_field: float32 [2, 4096, 8192], P(None, 'row', 'col'), may hold values from -5 to 5
- probe: float32 [2, 256, 256], replicated, may hold values from -6 to 6
- intensity: float32 [1536, 256, 256], P(('row', 'col')), may hold values from 0 to 4
- centers: int32 [1536, 2], P(('row', 'col')), may hold values from 0 to 8191, as said below
- picked: int32 [1536], P(('row', 'col')), may hold values 0 or 1
Outputs:
- object_out: float32 [2, 4096, 8192], P(None, 'row', 'col')
- probe_out: float32 [2, 256, 256], replicated
Inputs may be any that keep to these rules, and one draw needn't show every extreme that they name: `centers`: the frames f with k * 12 <= f < (k + 1) * 12 belong to subdomain k = 16 i + j: their centres lie in rows i * 512 to (i + 1) * 512 - 1 and columns j * 512 to (j + 1) * 512 - 1. Of one subdomain's frames at most 6 have centres in any one quarter of it (upper or lower 512/2 rows times left or right 512/2 columns), and in every subdomain some quarter holds exactly 6.
All inputs are finite; a program needn't handle non-finite values. No bound on the sum of `picked` on one device may be relied on, other than what follows from the above.
Results may differ from a plain program's by a relative error of at most 0.012.
The roundings to bfloat16 on the way count: a program that leaves them out, or rounds other values in their place, can miss the bound.
Values sent between devices are 32-bit elements; how exact they have to be, the bound alone decides.
No kernel may reach another device: no remote copies, remote signals or barrier semaphores. Data moves between devices by JAX's collectives and lax.ppermute only.
A program may use at most 128 MiB of HBM per device.

v0:
```python
import math

import jax
import jax.numpy as jnp
from jax import lax
from jax.sharding import PartitionSpec as P

ITERS = 2


object_rate = 0.02
probe_gain = 4.0


def padded_2(array, sides, width):
    for axis, dim in sides:
        count, length = (lax.axis_size(axis), array.shape[dim])
        up = [(i, (i + 1) % count) for i in range(count)]
        down = [(j, i) for i, j in up]
        last = lax.slice_in_dim(array, length - width, length, axis=dim)
        initial = lax.slice_in_dim(array, 0, width, axis=dim)
        before = lax.ppermute(last, axis, up)
        after = lax.ppermute(initial, axis, down)
        array = jnp.concatenate([before, array, after], axis=dim)
    return array


def from_behind(array, axis, by):
    count = lax.axis_size(axis)
    return lax.ppermute(array, axis, [(i, (i + by) % count) for i in range(count)])


def tables(frame_side):
    indices = jnp.arange(frame_side, dtype=jnp.int32)
    product = indices[:, None] * indices[None, :] % frame_side
    angle = product.astype(jnp.float32) * (2.0 * math.pi / frame_side)
    scale = 1.0 / math.sqrt(frame_side)
    real_part = (jnp.cos(angle) * scale).astype(jnp.bfloat16)
    imag_part = (-jnp.sin(angle) * scale).astype(jnp.bfloat16)
    right_mat = jnp.concatenate(
        [jnp.concatenate([real_part, imag_part], 1), jnp.concatenate([-imag_part, real_part], 1)], 0
    )
    left_mat = jnp.concatenate(
        [jnp.concatenate([real_part, -imag_part], 1), jnp.concatenate([imag_part, real_part], 1)], 0
    )
    return (right_mat, left_mat)


def frame_terms(windows, probe_now, intens, chosen, right_mat, left_mat):
    frame_side = probe_now.shape[-1]
    probe_re, probe_im = (probe_now[0], probe_now[1])
    window_re, window_im = (windows[:, 0], windows[:, 1])
    exit_re = probe_re * window_re - probe_im * window_im
    exit_im = probe_re * window_im + probe_im * window_re
    flat_exit = jnp.concatenate([exit_re, exit_im], axis=2).astype(jnp.bfloat16)
    partial_wave = jnp.einsum(
        "nab,bc->nac", flat_exit, right_mat, preferred_element_type=jnp.float32
    ).astype(jnp.bfloat16)
    stacked = jnp.concatenate(
        [partial_wave[:, :, :frame_side], partial_wave[:, :, frame_side:]], axis=1
    )
    farfield = jnp.einsum("ab,nbc->nac", left_mat, stacked, preferred_element_type=jnp.float32)
    far_re, far_im = (farfield[:, :frame_side], farfield[:, frame_side:])
    mismatch = (far_re * far_re + far_im * far_im - intens) * chosen.astype(jnp.float32)[
        :, None, None
    ]
    weighted = jnp.concatenate([mismatch * far_re, mismatch * far_im], axis=1).astype(jnp.bfloat16)
    returned = jnp.einsum(
        "ab,nbc->nac", right_mat, weighted, preferred_element_type=jnp.float32
    ).astype(jnp.bfloat16)
    flat_back = jnp.concatenate([returned[:, :frame_side], returned[:, frame_side:]], axis=2)
    gradient = jnp.einsum("nab,bc->nac", flat_back, left_mat, preferred_element_type=jnp.float32)
    grad_re, grad_im = (gradient[..., :frame_side], gradient[..., frame_side:])
    object_re = probe_re * grad_re + probe_im * grad_im
    object_im = probe_re * grad_im - probe_im * grad_re
    probe_re_sum = jnp.sum(window_re * grad_re + window_im * grad_im, axis=0)
    probe_im_sum = jnp.sum(window_re * grad_im - window_im * grad_re, axis=0)
    return (jnp.stack([object_re, object_im], axis=1), jnp.stack([probe_re_sum, probe_im_sum]))


def fold_axis(extended, axis, tile_side, frame_side):
    width = frame_side // 2
    middle = lax.slice_in_dim(extended, frame_side, frame_side + tile_side, axis=axis)
    leading = lax.slice_in_dim(extended, 0, width, axis=axis)
    trailing = lax.slice_in_dim(extended, tile_side + 3 * width, tile_side + 4 * width, axis=axis)
    lead_pad = [(0, 0)] * extended.ndim
    trail_pad = [(0, 0)] * extended.ndim
    lead_pad[axis] = (0, tile_side - width)
    trail_pad[axis] = (tile_side - width, 0)
    return middle + jnp.pad(leading, lead_pad) + jnp.pad(trailing, trail_pad)


def iterate(
    tile_now,
    probe_now,
    intens,
    centers,
    chosen,
    anchor_row,
    anchor_col,
    rows_all,
    cols_all,
    frames_total,
):
    frame_side = probe_now.shape[-1]
    tile_side = tile_now.shape[1]
    width = frame_side // 2
    right_mat, left_mat = tables(frame_side)
    local_row = (centers[:, 0] - anchor_row) % rows_all
    local_col = (centers[:, 1] - anchor_col) % cols_all
    slot_count = intens.shape[0]
    zero_index = jnp.zeros((), jnp.int32)
    for sweep in range(ITERS):
        padded = padded_2(tile_now, (("row", 1), ("col", 2)), width)
        windows = jax.vmap(
            lambda row_at, col_at: lax.dynamic_slice(
                padded, (zero_index, row_at, col_at), (2, frame_side, frame_side)
            )
        )(local_row, local_col)
        contrib, probe_part = frame_terms(windows, probe_now, intens, chosen, right_mat, left_mat)

        def add_slot(slot, gathered):
            corner = (zero_index, local_row[slot], local_col[slot])
            current = lax.dynamic_slice(gathered, corner, (2, frame_side, frame_side))
            return lax.dynamic_update_slice(gathered, current + contrib[slot], corner)

        gradient = lax.fori_loop(0, slot_count, add_slot, jnp.zeros(padded.shape, jnp.float32))
        outward = padded_2(gradient, (("row", 1), ("col", 2)), width)
        folded = fold_axis(fold_axis(outward, 1, tile_side, frame_side), 2, tile_side, frame_side)
        probe_total = lax.psum(probe_part, ("row", "col"))
        tile_now = tile_now - object_rate * folded
        probe_now = probe_now - probe_gain / frames_total * probe_total
    return (tile_now, probe_now)


def on_device(object_field, probe, intensity, centers, picked):
    tile_side = object_field.shape[1]
    half_side = tile_side // 2
    row_count = lax.axis_size("row")
    col_count = lax.axis_size("col")
    rows_all = tile_side * row_count
    cols_all = tile_side * col_count
    frames_total = intensity.shape[0] * row_count * col_count
    row_start = lax.axis_index("row") * tile_side
    col_start = lax.axis_index("col") * tile_side
    updated_tile, final_probe = iterate(
        object_field,
        probe,
        intensity,
        centers,
        picked,
        row_start,
        col_start,
        rows_all,
        cols_all,
        frames_total,
    )
    across = from_behind(updated_tile[:, :, :half_side], "col", -1)
    wide_tile = jnp.concatenate([updated_tile[:, :, half_side:], across], axis=2)
    below = from_behind(wide_tile[:, :half_side, :], "row", -1)
    final_tile = jnp.concatenate([wide_tile[:, half_side:, :], below], axis=1)
    return (final_tile, final_probe)


def solution(mesh):
    in_specs = (
        P(None, "row", "col"),
        P(),
        P(("row", "col"), None, None),
        P(("row", "col"), None),
        P(("row", "col")),
    )
    out_specs = (P(None, "row", "col"), P())
    return jax.shard_map(
        on_device, mesh=mesh, in_specs=in_specs, out_specs=out_specs, check_vma=False
    )
```

profile of v0, /device:TPU:1, one launch (start us, length us, event | category | flops | bytes accessed | tf_op | source)
XLA Modules:
  0.0 1005.1 jit_solution(3924710727894133087)
XLA Ops:
  16.6 17.5 %collective-permute-done = f32[2,128,512]{2,1,0:T(8,128)} collective-permute-done((f32[2,128,512]{2,1,0:T(8,128)}, f32[2,128,512]{2,1,0:T(8,128)}, u32[]{:S(2)}, u32[]{:S(2)}) %collective-permute-start) | collective-permute-done | bytes 524320 | tf_op jit(solution)/shard_map/ppermute | solution.py:22
  58.6 48.9 %while.30 = (s32[]{:T(128)}, f32[2,768,768]{2,1,0:T(8,128)}, s32[12,3]{0,1:T(4,128)S(1)}, f32[12,2,256,256]{3,2,0,1:T(8,128)}, s32[]{:T(128)}) while((s32[]{:T(128)}, f32[2,768,768]{2,1,0:T(8,128)}, s32[12,3]{0,1:T(4,128)S(1)}, f32[12,2,256,256]{3,2,0,1:T(8,128)}, s32[]{:T(128)}) %tuple.116), condition=%wide.while_cond, body=%wide.while_body.sunk | while | flops 2 | bytes 1050217 | solution.py:116
  129.7 158.6 %while.28 = (s32[]{:T(128)}, f32[2,768,768]{2,1,0:T(8,128)}, s32[12]{0:T(128)S(1)}, s32[12]{0:T(128)S(1)}, f32[12,2,256,256]{3,2,0,1:T(8,128)}, /*index=5*/s32[]{:T(128)}, s32[]{:T(128)}, s32[]{:T(128)}) while((s32[]{:T(128)}, f32[2,768,768]{2,1,0:T(8,128)}, s32[12]{0:T(128)S(1)}, s32[12]{0:T(128)S(1)}, f32[12,2,256,256]{3,2,0,1:T(8,128)}, ...), condition=%wide.region_1.2_spmd, body=%wide.region_0.1_spmd.sunk | while | flops 131080 | bytes 2621633 | solution.py:127
  136.3 6.8 dynamic_update_slice.16
  149.6 6.5 dynamic_update_slice.16
  175.7 6.8 dynamic_update_slice.16
  189.1 6.5 dynamic_update_slice.16
  202.2 6.8 dynamic_update_slice.16
  215.6 6.6 dynamic_update_slice.16
  228.8 6.8 dynamic_update_slice.16
  242.2 6.8 dynamic_update_slice.16
  255.6 6.5 dynamic_update_slice.16
  281.5 6.8 dynamic_update_slice.16
  293.8 29.0 %collective-permute-done.4 = f32[2,128,768]{2,1,0:T(8,128)S(1)} collective-permute-done((f32[2,128,768]{2,1,0:T(8,128)S(1)}, f32[2,128,768]{2,1,0:T(8,128)S(1)}, u32[]{:S(2)}, u32[]{:S(2)}) %collective-permute-start.4) | collective-permute-done | bytes 786464 | tf_op jit(solution)/shard_map/ppermute | solution.py:22
  329.2 11.7 %collective-permute-done.6 = f32[2,1024,128]{2,1,0:T(8,128)S(1)} collective-permute-done((f32[2,1024,128]{2,1,0:T(8,128)S(1)}, f32[2,1024,128]{2,1,0:T(8,128)S(1)}, u32[]{:S(2)}, u32[]{:S(2)}) %collective-permute-start.6) | collective-permute-done | bytes 1048608 | tf_op jit(solution)/shard_map/ppermute | solution.py:22
  350.9 16.7 %collective-permute-done.8 = f32[2,128,512]{2,1,0:T(8,128)S(1)} collective-permute-done((f32[2,128,512]{2,1,0:T(8,128)S(1)}, f32[2,128,512]{2,1,0:T(8,128)S(1)}, u32[]{:S(2)}, u32[]{:S(2)}) %collective-permute-start.8) | collective-permute-done | bytes 524320 | tf_op jit(solution)/shard_map/ppermute | solution.py:22
  375.3 148.6 %all-reduce.7.cloned.1.call-done = f32[2,256,256]{2,1,0:T(8,128)} async-done(((f32[2,256,256]{2,1,0:T(8,128)}), f32[2,256,256]{2,1,0:T(8,128)}) %all-reduce.7.cloned.1.call-update) | async-done | bytes 524304 | tf_op jit(solution)/shard_map/psum | solution.py:130
  532.3 48.8 %while.31 = (s32[]{:T(128)}, f32[2,768,768]{2,1,0:T(8,128)}, s32[12,3]{0,1:T(4,128)S(1)}, f32[12,2,256,256]{3,2,0,1:T(8,128)}, s32[]{:T(128)}) while((s32[]{:T(128)}, f32[2,768,768]{2,1,0:T(8,128)}, s32[12,3]{0,1:T(4,128)S(1)}, f32[12,2,256,256]{3,2,0,1:T(8,128)}, s32[]{:T(128)}) %tuple.132), condition=%wide.while_cond.1, body=%wide.while_body.1.sunk | while | flops 2 | bytes 1050217 | solution.py:116
  603.4 158.8 %while.29 = (s32[]{:T(128)}, f32[2,768,768]{2,1,0:T(8,128)}, s32[12]{0:T(128)S(1)}, s32[12]{0:T(128)S(1)}, f32[12,2,256,256]{3,2,0,1:T(8,128)}, /*index=5*/s32[]{:T(128)}, s32[]{:T(128)}, s32[]{:T(128)}) while((s32[]{:T(128)}, f32[2,768,768]{2,1,0:T(8,128)}, s32[12]{0:T(128)S(1)}, s32[12]{0:T(128)S(1)}, f32[12,2,256,256]{3,2,0,1:T(8,128)}, ...), condition=%wide.region_6.7_spmd, body=%wide.region_5.6_spmd.sunk | while | flops 131080 | bytes 2621633 | solution.py:127
  610.2 6.8 dynamic_update_slice.17
  649.6 6.8 dynamic_update_slice.17
  663.0 6.5 dynamic_update_slice.17
  676.2 6.8 dynamic_update_slice.17
  689.5 6.6 dynamic_update_slice.17
  702.7 6.8 dynamic_update_slice.17
  716.1 6.8 dynamic_update_slice.17
  729.5 6.5 dynamic_update_slice.17
  755.4 6.8 dynamic_update_slice.17
  767.5 28.5 %collective-permute-done.12 = f32[2,128,768]{2,1,0:T(8,128)S(1)} collective-permute-done((f32[2,128,768]{2,1,0:T(8,128)S(1)}, f32[2,128,768]{2,1,0:T(8,128)S(1)}, u32[]{:S(2)}, u32[]{:S(2)}) %collective-permute-start.12) | collective-permute-done | bytes 786464 | tf_op jit(solution)/shard_map/ppermute | solution.py:22
  802.0 10.9 %collective-permute-done.14 = f32[2,1024,128]{2,1,0:T(8,128)S(1)} collective-permute-done((f32[2,1024,128]{2,1,0:T(8,128)S(1)}, f32[2,1024,128]{2,1,0:T(8,128)S(1)}, u32[]{:S(2)}, u32[]{:S(2)}) %collective-permute-start.14) | collective-permute-done | bytes 1048608 | tf_op jit(solution)/shard_map/ppermute | solution.py:22
  823.4 10.1 %collective-permute-done.16 = f32[2,512,256]{2,1,0:T(8,128)S(1)} collective-permute-done((f32[2,512,256]{2,1,0:T(8,128)S(1)}, f32[2,512,256]{2,1,0:T(8,128)S(1)}, u32[]{:S(2)}, u32[]{:S(2)}) %collective-permute-start.16) | collective-permute-done | bytes 1048608 | tf_op jit(solution)/shard_map/ppermute | solution.py:30
  838.1 156.6 %all-reduce.9.cloned.1.call-done = f32[2,256,256]{2,1,0:T(8,128)} async-done(((f32[2,256,256]{2,1,0:T(8,128)}), f32[2,256,256]{2,1,0:T(8,128)}) %all-reduce.9.cloned.1.call-update) | async-done | bytes 524304 | tf_op jit(solution)/shard_map/psum | solution.py:130
  (300 shorter events, 339.8 us)
Async XLA Ops:
  7.2 516.8 %all-reduce.7.cloned.1.call-start = ((), (), s32[]{:S(2)}) async-start(), calls=%async_computation | async-start | bytes 1048576 | tf_op jit(solution)/shard_map/psum | solution.py:130
  9.4 24.6 %collective-permute-start = (f32[2,128,512]{2,1,0:T(8,128)}, f32[2,128,512]{2,1,0:T(8,128)}, u32[]{:S(2)}, u32[]{:S(2)}) collective-permute-start(f32[2,128,512]{2,1,0:T(8,128)} %get-tuple-element.305), channel_id=1, source_target_pairs={{0,16},{16,32},{32,48},{48,64},{64,80},{80,96},{96,112},{112,0},{1... | collective-permute-start | bytes 1572872 | tf_op jit(solution)/shard_map/ppermute | solution.py:22
  11.9 25.0 %collective-permute-start.1 = (f32[2,128,512]{2,1,0:T(8,128)}, f32[2,128,512]{2,1,0:T(8,128)}, u32[]{:S(2)}, u32[]{:S(2)}) collective-permute-start(f32[2,128,512]{2,1,0:T(8,128)} %get-tuple-element.304), channel_id=1, source_target_pairs={{16,0},{32,16},{48,32},{64,48},{80,64},{96,80},{112,96},{0,112},{1... | collective-permute-start | bytes 1572872 | tf_op jit(solution)/shard_map/ppermute | solution.py:23
  16.5 99.0 %copy-start.2 = (f32[12,256,256]{1,2,0:T(8,128)}, f32[12,256,256]{1,2,0:T(8,128)S(1)}, u32[]{:S(2)}) copy-start(f32[12,256,256]{1,2,0:T(8,128)S(1)} %copy.10) | copy-start | bytes 9437188
  36.9 7.2 copy-start.8
  38.2 11.7 %collective-permute-start.2 = (f32[2,768,128]{2,1,0:T(8,128)S(1)}, f32[2,768,128]{2,1,0:T(8,128)S(1)}, u32[]{:S(2)}, u32[]{:S(2)}) collective-permute-start(f32[2,768,128]{2,1,0:T(8,128)S(1)} %get-tuple-element.296), channel_id=1, source_target_pairs={{0,1},{1,2},{2,3},{3,4},{4,5},{5,6},{6,7},{7,8},{8,9},{9,10},{10,1... | collective-permute-start | bytes 2359304 | tf_op jit(solution)/shard_map/ppermute | solution.py:22
  41.0 11.7 %collective-permute-start.3 = (f32[2,768,128]{2,1,0:T(8,128)S(1)}, f32[2,768,128]{2,1,0:T(8,128)S(1)}, u32[]{:S(2)}, u32[]{:S(2)}) collective-permute-start(f32[2,768,128]{2,1,0:T(8,128)S(1)} %get-tuple-element.297), channel_id=1, source_target_pairs={{1,0},{2,1},{3,2},{4,3},{5,4},{6,5},{7,6},{8,7},{9,8},{10,9},{11,1... | collective-permute-start | bytes 2359304 | tf_op jit(solution)/shard_map/ppermute | solution.py:23
  107.6 3.8 copy-start.11
  107.6 3.8 copy-start.13
  288.2 34.9 %copy-start.17 = (s32[12]{0:T(128)}, s32[12]{0:T(128)S(1)}, u32[]{:S(2)}) copy-start(s32[12]{0:T(128)S(1)} %get-tuple-element.551) | copy-start | bytes 148
  288.2 34.6 %copy-start.1 = (f32[2,768,768]{2,1,0:T(8,128)S(1)}, f32[2,768,768]{2,1,0:T(8,128)}, u32[]{:S(2)}) copy-start(f32[2,768,768]{2,1,0:T(8,128)} %get-tuple-element.190) | copy-start | bytes 14155780
  289.9 32.9 %collective-permute-start.4 = (f32[2,128,768]{2,1,0:T(8,128)S(1)}, f32[2,128,768]{2,1,0:T(8,128)S(1)}, u32[]{:S(2)}, u32[]{:S(2)}) collective-permute-start(f32[2,128,768]{2,1,0:T(8,128)S(1)} %get-tuple-element.285), channel_id=1, source_target_pairs={{0,16},{16,32},{32,48},{48,64},{64,80},{80,96},{96,112},{112,0},{1... | collective-permute-start | bytes 2359304 | tf_op jit(solution)/shard_map/ppermute | solution.py:22
  291.4 36.1 %collective-permute-start.5 = (f32[2,128,768]{2,1,0:T(8,128)S(1)}, f32[2,128,768]{2,1,0:T(8,128)S(1)}, u32[]{:S(2)}, u32[]{:S(2)}) collective-permute-start(f32[2,128,768]{2,1,0:T(8,128)S(1)} %get-tuple-element.284), channel_id=1, source_target_pairs={{16,0},{32,16},{48,32},{64,48},{80,64},{96,80},{112,96},{0,112},{1... | collective-permute-start | bytes 2359304 | tf_op jit(solution)/shard_map/ppermute | solution.py:23
  327.8 13.2 %collective-permute-start.6 = (f32[2,1024,128]{2,1,0:T(8,128)S(1)}, f32[2,1024,128]{2,1,0:T(8,128)S(1)}, u32[]{:S(2)}, u32[]{:S(2)}) collective-permute-start(f32[2,1024,128]{2,1,0:T(8,128)S(1)} %get-tuple-element.280), channel_id=1, source_target_pairs={{0,1},{1,2},{2,3},{3,4},{4,5},{5,6},{6,7},{7,8},{8,9},{9,10},{10,1... | collective-permute-start | bytes 3145736 | tf_op jit(solution)/shard_map/ppermute | solution.py:22
  329.2 15.5 %copy-start.15 = (pred[512]{0:T(512)(128)(4,1)S(1)}, pred[512]{0:T(512)(128)(4,1)}, u32[]{:S(2)}) copy-start(pred[512]{0:T(512)(128)(4,1)} %constant.130.clone.1) | copy-start | bytes 1540
  329.2 14.5 %collective-permute-start.7 = (f32[2,1024,128]{2,1,0:T(8,128)S(1)}, f32[2,1024,128]{2,1,0:T(8,128)S(1)}, u32[]{:S(2)}, u32[]{:S(2)}) collective-permute-start(f32[2,1024,128]{2,1,0:T(8,128)S(1)} %get-tuple-element.281), channel_id=1, source_target_pairs={{1,0},{2,1},{3,2},{4,3},{5,4},{6,5},{7,6},{8,7},{9,8},{10,9},{11,1... | collective-permute-start | bytes 3145736 | tf_op jit(solution)/shard_map/ppermute | solution.py:23
  347.2 20.4 %collective-permute-start.8 = (f32[2,128,512]{2,1,0:T(8,128)S(1)}, f32[2,128,512]{2,1,0:T(8,128)S(1)}, u32[]{:S(2)}, u32[]{:S(2)}) collective-permute-start(f32[2,128,512]{2,1,0:T(8,128)S(1)} %get-tuple-element.302), channel_id=1, source_target_pairs={{0,16},{16,32},{32,48},{48,64},{64,80},{80,96},{96,112},{112,0},{1... | collective-permute-start | bytes 1572872 | tf_op jit(solution)/shard_map/ppermute | solution.py:22
  347.3 176.6 %copy-start.9 = (f32[2,256,256]{2,1,0:T(8,128)S(1)}, f32[2,256,256]{2,1,0:T(8,128)}, u32[]{:S(2)}) copy-start(f32[2,256,256]{2,1,0:T(8,128)} %param.10) | copy-start | bytes 1572868
  347.3 23.2 %collective-permute-start.9 = (f32[2,128,512]{2,1,0:T(8,128)S(1)}, f32[2,128,512]{2,1,0:T(8,128)S(1)}, u32[]{:S(2)}, u32[]{:S(2)}) collective-permute-start(f32[2,128,512]{2,1,0:T(8,128)S(1)} %get-tuple-element.303), channel_id=1, source_target_pairs={{16,0},{32,16},{48,32},{64,48},{80,64},{96,80},{112,96},{0,112},{1... | collective-permute-start | bytes 1572872 | tf_op jit(solution)/shard_map/ppermute | solution.py:23
  371.9 153.2 %collective-permute-start.10 = (f32[2,768,128]{2,1,0:T(8,128)}, f32[2,768,128]{2,1,0:T(8,128)}, u32[]{:S(2)}, u32[]{:S(2)}) collective-permute-start(f32[2,768,128]{2,1,0:T(8,128)} %get-tuple-element.290), channel_id=1, source_target_pairs={{0,1},{1,2},{2,3},{3,4},{4,5},{5,6},{6,7},{7,8},{8,9},{9,10},{10,1... | collective-permute-start | bytes 2359304 | tf_op jit(solution)/shard_map/ppermute | solution.py:22
  373.1 152.0 %collective-permute-start.11 = (f32[2,768,128]{2,1,0:T(8,128)}, f32[2,768,128]{2,1,0:T(8,128)}, u32[]{:S(2)}, u32[]{:S(2)}) collective-permute-start(f32[2,768,128]{2,1,0:T(8,128)} %get-tuple-element.291), channel_id=1, source_target_pairs={{1,0},{2,1},{3,2},{4,3},{5,4},{6,5},{7,6},{8,7},{9,8},{10,9},{11,1... | collective-permute-start | bytes 2359304 | tf_op jit(solution)/shard_map/ppermute | solution.py:23
  375.2 619.4 %all-reduce.9.cloned.1.call-start = ((), (), s32[]{:S(2)}) async-start(), calls=%async_computation.1 | async-start | bytes 1048576 | tf_op jit(solution)/shard_map/psum | solution.py:130
  581.1 3.8 copy-start.12
  581.1 3.8 copy-start.14
  762.2 33.9 %copy-start = (f32[2,768,768]{2,1,0:T(8,128)S(1)}, f32[2,768,768]{2,1,0:T(8,128)}, u32[]{:S(2)}) copy-start(f32[2,768,768]{2,1,0:T(8,128)} %get-tuple-element.191) | copy-start | bytes 14155780
  763.9 32.2 %collective-permute-start.12 = (f32[2,128,768]{2,1,0:T(8,128)S(1)}, f32[2,128,768]{2,1,0:T(8,128)S(1)}, u32[]{:S(2)}, u32[]{:S(2)}) collective-permute-start(f32[2,128,768]{2,1,0:T(8,128)S(1)} %get-tuple-element.283), channel_id=1, source_target_pairs={{0,16},{16,32},{32,48},{48,64},{64,80},{80,96},{96,112},{112,0},{1... | collective-permute-start | bytes 2359304 | tf_op jit(solution)/shard_map/ppermute | solution.py:22
  763.9 35.9 %collective-permute-start.13 = (f32[2,128,768]{2,1,0:T(8,128)S(1)}, f32[2,128,768]{2,1,0:T(8,128)S(1)}, u32[]{:S(2)}, u32[]{:S(2)}) collective-permute-start(f32[2,128,768]{2,1,0:T(8,128)S(1)} %get-tuple-element.282), channel_id=1, source_target_pairs={{16,0},{32,16},{48,32},{64,48},{80,64},{96,80},{112,96},{0,112},{1... | collective-permute-start | bytes 2359304 | tf_op jit(solution)/shard_map/ppermute | solution.py:23
  800.0 12.8 %collective-permute-start.14 = (f32[2,1024,128]{2,1,0:T(8,128)S(1)}, f32[2,1024,128]{2,1,0:T(8,128)S(1)}, u32[]{:S(2)}, u32[]{:S(2)}) collective-permute-start(f32[2,1024,128]{2,1,0:T(8,128)S(1)} %get-tuple-element.276), channel_id=1, source_target_pairs={{0,1},{1,2},{2,3},{3,4},{4,5},{5,6},{6,7},{7,8},{8,9},{9,10},{10,1... | collective-permute-start | bytes 3145736 | tf_op jit(solution)/shard_map/ppermute | solution.py:22
  801.1 14.5 %collective-permute-start.15 = (f32[2,1024,128]{2,1,0:T(8,128)S(1)}, f32[2,1024,128]{2,1,0:T(8,128)S(1)}, u32[]{:S(2)}, u32[]{:S(2)}) collective-permute-start(f32[2,1024,128]{2,1,0:T(8,128)S(1)} %get-tuple-element.277), channel_id=1, source_target_pairs={{1,0},{2,1},{3,2},{4,3},{5,4},{6,5},{7,6},{8,7},{9,8},{10,9},{11,1... | collective-permute-start | bytes 3145736 | tf_op jit(solution)/shard_map/ppermute | solution.py:23
  819.2 18.0 %copy-start.10 = (f32[256,256]{1,0:T(8,128)S(1)}, f32[256,256]{1,0:T(8,128)}, u32[]{:S(2)}) copy-start(f32[256,256]{1,0:T(8,128)} %get-tuple-element.219) | copy-start | bytes 786436
  819.2 14.3 %collective-permute-start.16 = (f32[2,512,256]{2,1,0:T(8,128)S(1)}, f32[2,512,256]{2,1,0:T(8,128)S(1)}, u32[]{:S(2)}, u32[]{:S(2)}) collective-permute-start(f32[2,512,256]{2,1,0:T(8,128)S(1)} %get-tuple-element.301), channel_id=1, source_target_pairs={{0,15},{1,0},{2,1},{3,2},{4,3},{5,4},{6,5},{7,6},{8,7},{9,8},{10,9... | collective-permute-start | bytes 3145736 | tf_op jit(solution)/shard_map/ppermute | solution.py:30
  834.8 161.8 %collective-permute-start.17 = (f32[2,256,512]{2,1,0:T(8,128)}, f32[2,256,512]{2,1,0:T(8,128)S(1)}, u32[]{:S(2)}, u32[]{:S(2)}) collective-permute-start(f32[2,256,512]{2,1,0:T(8,128)} %get-tuple-element.299), channel_id=1, source_target_pairs={{0,112},{16,0},{32,16},{48,32},{64,48},{80,64},{96,80},{112,96},{1... | collective-permute-start | bytes 3145736 | tf_op jit(solution)/shard_map/ppermute | solution.py:30
  (12 other events, 27.7 us)
Sparse Core Ops, SparseCore 0:
  375.4 148.5 all-reduce.6
  838.2 156.4 all-reduce.8
where the time goes:
time: 1020 us; the launch traced here: 1010 us
  waiting for transfers between devices  454 us (45%)
  local copies, waits for them, and re-layouts  313 us (31%)
  loops' own time  93.7 us (9%)
  other arithmetic  82.9 us (8%)
  starting transfers between devices  31.1 us (3%)
  matrix products  15.2 us (1%)
  between operations  14.9 us (1%)
    psum x2, waiting for transfers between devices, iterate(): probe_total = lax.psum(probe_part, ('row', 'col'))  305 us
    dynamic_update_slice x24, local copies, waits for them, and re-layouts, add_slot(): return lax.dynamic_update_slice(gathered, current + contrib[slot], corner)  159 us
    ppermute x8, waiting for transfers between devices, padded_2(): before = lax.ppermute(last, axis, up)  119 us
    gather x72, local copies, waits for them, and re-layouts  97.7 us
    another operation x2, loops' own time, iterate(): lax.fori_loop(0, slot_count, add_slot, jnp.zeros(padded.shape, jnp.float32))  93.6 us
    add x24, other arithmetic, add_slot(): return lax.dynamic_update_slice(gathered, current + contrib[slot], corner)  36.8 us
    dynamic_slice x48, local copies, waits for them, and re-layouts, add_slot(): corner = (zero_index, local_row[slot], local_col[slot])  28.1 us
  transfers between devices with their start and end apart: 20, of which 16 were waited for; matrix products, arithmetic and copies ran while one was open for 1% of the time, Pallas kernels for 0%

commit v1 on v0

v1 whole, which is shorter than its diff:
```python
import math

import jax
import jax.numpy as jnp
import numpy as np
from jax import lax
from jax.experimental import pallas as pl
from jax.experimental.pallas import tpu as pltpu
from jax.sharding import PartitionSpec as P

ITERS = 2


object_rate = 0.02
probe_gain = 4.0
LANES = 128
SUBLANES = 8


def tables(frame_side):
    indices = np.arange(frame_side)
    angle = (indices[:, None] * indices[None, :] % frame_side) * (2.0 * math.pi / frame_side)
    scale = 1.0 / math.sqrt(frame_side)
    real_part = (np.cos(angle) * scale).astype(np.float32).astype(jnp.bfloat16)
    imag_part = (-np.sin(angle) * scale).astype(np.float32).astype(jnp.bfloat16)
    right_mat = np.block([[real_part, imag_part], [-imag_part, real_part]])
    left_mat = np.block([[real_part, -imag_part], [imag_part, real_part]])
    return (jnp.asarray(right_mat), jnp.asarray(left_mat))


def frames_kernel(places, out_cols, side, info, *refs):
    count = len(places)
    pieces = refs[:count]
    probe, intens, right_mat, left_mat = refs[count : count + 4]
    outs = refs[count + 4 : count + 4 + len(out_cols)]
    probe_grad, region, grad, held, chosen = refs[count + 4 + len(out_cols) :]
    for piece, (row_at, col_at) in zip(pieces, places):
        rows, cols = piece.shape[1:]
        region[:, row_at : row_at + rows, col_at : col_at + cols] = piece[...]
    grad[...] = jnp.zeros_like(grad)
    probe_grad[...] = jnp.zeros_like(probe_grad)

    def pick(slot, found):
        @pl.when(info[slot, 2] != 0)
        def _():
            chosen[found] = slot

        return found + jnp.where(info[slot, 2] != 0, 1, 0)

    total = lax.fori_loop(0, info.shape[0], pick, jnp.int32(0))
    lane = lax.broadcasted_iota(jnp.int32, (side + SUBLANES, LANES), 1)
    line = lax.broadcasted_iota(jnp.int32, (1, SUBLANES, LANES), 1)

    def one_frame(at, carried):
        slot = chosen[at]
        row_at = info[slot, 0]
        col_at = info[slot, 1]
        col_base = pl.multiple_of(col_at // LANES * LANES, LANES)
        row_base = pl.multiple_of(row_at // SUBLANES * SUBLANES, SUBLANES)
        col_shift = col_at - col_base
        row_shift = row_at - row_base
        col_back = jnp.where(col_shift == 0, 0, LANES - col_shift)
        row_back = jnp.where(row_shift == 0, 0, SUBLANES - row_shift)
        rows = pl.ds(row_base, side + SUBLANES)
        tiles = side // SUBLANES
        inside = lane < LANES - col_shift
        inside_row = line < SUBLANES - row_shift

        def window(part):
            turned = [
                pltpu.roll(region[part, rows, pl.ds(pl.multiple_of(col_base + LANES * k, LANES), LANES)], col_back, 1)
                for k in range(3)
            ]
            for k in range(2):
                piece = jnp.where(inside, turned[k], turned[k + 1]).reshape(tiles + 1, SUBLANES, LANES)
                piece = pltpu.roll(piece, row_back, 1)
                piece = jnp.where(inside_row, piece[:tiles], piece[1:]).reshape(side, LANES)
                held[part, :, k * LANES : (k + 1) * LANES] = piece

        window(0)
        window(1)
        win_re, win_im = held[0], held[1]
        pr_re, pr_im = probe[0], probe[1]
        exit_re = pr_re * win_re - pr_im * win_im
        exit_im = pr_re * win_im + pr_im * win_re
        flat = jnp.concatenate([exit_re, exit_im], axis=1).astype(jnp.bfloat16)
        wave = jnp.dot(flat, right_mat[...], preferred_element_type=jnp.float32).astype(jnp.bfloat16)
        stacked = jnp.concatenate([wave[:, :side], wave[:, side:]], axis=0)
        far = jnp.dot(left_mat[...], stacked, preferred_element_type=jnp.float32)
        far_re, far_im = far[:side], far[side:]
        mismatch = far_re * far_re + far_im * far_im - intens[slot]
        weighted = jnp.concatenate([mismatch * far_re, mismatch * far_im], axis=0).astype(jnp.bfloat16)
        returned = jnp.dot(right_mat[...], weighted, preferred_element_type=jnp.float32).astype(jnp.bfloat16)
        flat_back = jnp.concatenate([returned[:side], returned[side:]], axis=1)
        gradient = jnp.dot(flat_back, left_mat[...], preferred_element_type=jnp.float32)
        gr_re, gr_im = gradient[:, :side], gradient[:, side:]
        win_re, win_im = held[0], held[1]
        probe_grad[0] += win_re * gr_re + win_im * gr_im
        probe_grad[1] += win_re * gr_im - win_im * gr_re
        outside = lane >= col_shift
        outside_row = line >= row_shift
        nothing = jnp.zeros((1, SUBLANES, LANES), jnp.float32)

        def spread(part, value):
            turned = []
            for k in range(2):
                piece = value[:, k * LANES : (k + 1) * LANES].reshape(tiles, SUBLANES, LANES)
                piece = pltpu.roll(piece, row_shift, 1)
                piece = jnp.where(
                    outside_row,
                    jnp.concatenate([piece, nothing], axis=0),
                    jnp.concatenate([nothing, piece], axis=0),
                ).reshape(side + SUBLANES, LANES)
                turned.append(pltpu.roll(piece, col_shift, 1))
            first, second = turned
            grad[part, rows, pl.ds(col_base, LANES)] += jnp.where(outside, first, 0.0)
            grad[part, rows, pl.ds(pl.multiple_of(col_base + LANES, LANES), LANES)] += jnp.where(outside, second, first)
            grad[part, rows, pl.ds(pl.multiple_of(col_base + 2 * LANES, LANES), LANES)] += jnp.where(outside, 0.0, second)

        spread(0, pr_re * gr_re + pr_im * gr_im)
        spread(1, pr_re * gr_im - pr_im * gr_re)
        return carried

    lax.fori_loop(0, total, one_frame, 0)
    for out, (first, last) in zip(outs, out_cols):
        out[...] = grad[:, :, first:last]


def frames(info, pieces, places, probe, intensity, mats, rows, cols, out_cols):
    side = probe.shape[-1]
    vmem = pl.BlockSpec(memory_space=pltpu.VMEM)
    smem = pl.BlockSpec(memory_space=pltpu.SMEM)
    out_shapes = [jax.ShapeDtypeStruct((2, rows, last - first), jnp.float32) for first, last in out_cols]
    out_shapes.append(jax.ShapeDtypeStruct(probe.shape, jnp.float32))

    def kernel(*refs):
        frames_kernel(places, out_cols, side, *refs)

    return pl.pallas_call(
        kernel,
        out_shape=out_shapes,
        in_specs=[smem] + [vmem] * (len(pieces) + 4),
        out_specs=[vmem] * len(out_shapes),
        scratch_shapes=[
            pltpu.VMEM((2, rows, cols), jnp.float32),
            pltpu.VMEM((2, rows, cols), jnp.float32),
            pltpu.VMEM(probe.shape, jnp.float32),
            pltpu.SMEM((info.shape[0],), jnp.int32),
        ],
        compiler_params=pltpu.CompilerParams(vmem_limit_bytes=56 * 1024 * 1024),
        name="frames",
    )(info, *pieces, probe, intensity, *mats)


def shifted(array, axis, by):
    count = lax.axis_size(axis)
    return lax.ppermute(array, axis, [(i, (i + by) % count) for i in range(count)])


def probe_sum(part, shape):
    row_count, col_count = lax.axis_size("row"), lax.axis_size("col")
    x_count, lo_count, core_count = row_count // 2, 2, 2
    y_count, hi_count = col_count // 4, 2
    z_count = lo_count * hi_count

    def place(x, z, y, core):
        return (x * lo_count + z % lo_count) * col_count + (z // lo_count) * (y_count * core_count) + y * core_count + core

    def moved(array, axis, by):
        pairs = []
        for x in range(x_count):
            for z in range(z_count):
                for y in range(y_count):
                    for core in range(core_count):
                        to = {"x": x, "z": z, "y": y, "core": core}
                        size = {"x": x_count, "z": z_count, "y": y_count, "core": core_count}[axis]
                        to[axis] = (to[axis] + by) % size
                        pairs.append((place(x, z, y, core), place(**to)))
        return lax.ppermute(array, ("row", "col"), pairs)

    col = lax.axis_index("col")
    core = col % core_count
    y = col // core_count % y_count
    flat = part.reshape(-1, shape[-1])
    halves = flat.reshape(core_count, -1, shape[-1])
    mine = lax.dynamic_index_in_dim(halves, core, 0, False)
    other = lax.dynamic_index_in_dim(halves, 1 - core, 0, False)
    mine = mine + moved(other, "core", 1)
    quarters = mine.reshape(y_count, -1, shape[-1])
    total = lax.dynamic_index_in_dim(quarters, y, 0, False)
    arrived = [
        moved(lax.dynamic_index_in_dim(quarters, (y + by) % y_count, 0, False), "y", by) for by in range(1, y_count)
    ]
    for value in arrived:
        total = total + value
    for axis, size in (("x", x_count), ("z", z_count)):
        arrived = [moved(total, axis, by) for by in range(1, size)]
        for value in arrived:
            total = total + value
    gathered = [total] + [moved(total, "y", by) for by in range(1, y_count)]
    half = jnp.zeros(quarters.shape, jnp.float32)
    for by, value in enumerate(gathered):
        half = lax.dynamic_update_index_in_dim(half, value, (y - by) % y_count, 0)
    half = half.reshape(mine.shape)
    other = moved(half, "core", 1)
    first = jnp.where(core == 0, half, other)
    second = jnp.where(core == 0, other, half)
    return jnp.concatenate([first, second], axis=0).reshape(shape)


def on_device(object_field, probe, intensity, centers, picked):
    tile = object_field.shape[1]
    side = probe.shape[-1]
    width = side // 2
    half = tile // 2
    full = tile + side
    rows_all = tile * lax.axis_size("row")
    cols_all = tile * lax.axis_size("col")
    frames_total = intensity.shape[0] * lax.axis_size("row") * lax.axis_size("col")
    mats = tables(side)
    local_row = (centers[:, 0] - lax.axis_index("row") * tile) % rows_all
    local_col = (centers[:, 1] - lax.axis_index("col") * tile) % cols_all
    info = jnp.stack([local_row, local_col, picked], axis=1)
    out_cols = ((0, width), (width, width + tile), (width + tile, full))

    below = shifted(object_field[:, :width], "row", -1)
    above = shifted(object_field[:, tile - width :], "row", 1)
    at_left = shifted(object_field[:, :, tile - width :], "col", 1)
    at_right = shifted(object_field[:, :, :width], "col", -1)
    ends = jnp.concatenate([above, below], axis=1)
    ends_left = shifted(ends[:, :, tile - width :], "col", 1)
    ends_right = shifted(ends[:, :, :width], "col", -1)
    left_old = jnp.concatenate([ends_left[:, :width], at_left, ends_left[:, width:]], axis=1)
    right_old = jnp.concatenate([ends_right[:, :width], at_right, ends_right[:, width:]], axis=1)
    centre_old = jnp.concatenate([above, object_field, below], axis=1)
    places = ((0, 0), (0, width), (0, width + tile))
    grad_left, grad_mid, grad_right, probe_part = frames(
        info, (left_old, centre_old, right_old), places, probe, intensity, mats, full, full, out_cols
    )

    probe_total = probe_sum(probe_part, probe.shape)
    from_right = shifted(grad_left, "col", -1)
    from_left = shifted(grad_right, "col", 1)
    inner_up = shifted(grad_mid[:, :side, width : tile - width], "row", -1)
    inner_down = shifted(grad_mid[:, tile:, width : tile - width], "row", 1)
    edge_left = grad_mid[:, :, :width] + from_left
    edge_right = grad_mid[:, :, tile - width :] + from_right
    edges = jnp.concatenate([edge_left, edge_right], axis=2)
    edges_up = shifted(edges[:, :side], "row", -1)
    edges_down = shifted(edges[:, tile:], "row", 1)
    gap = ((0, 0), (0, tile - side), (0, 0))
    add_edges = jnp.concatenate([edges_down, jnp.zeros((2, tile - side, 2 * width), jnp.float32), edges_up], axis=1)
    edges = edges + add_edges
    add_inner = jnp.concatenate([inner_down, jnp.zeros((2, tile - side, tile - side), jnp.float32), inner_up], axis=1)
    inner = grad_mid[:, :, width : tile - width] + add_inner
    folded = jnp.concatenate([edges[:, :, :width], inner, edges[:, :, width:]], axis=2)
    centre = centre_old - object_rate * folded
    left = shifted(centre[:, :, tile - width :], "col", 1)
    right = shifted(centre[:, :, :width], "col", -1)
    probe_now = probe - probe_gain / frames_total * probe_total

    grad_left, grad_mid, grad_right, probe_part = frames(
        info, (left, centre, right), places, probe_now, intensity, mats, full, full, out_cols
    )

    probe_total = probe_sum(probe_part, probe.shape)
    own = jnp.pad(centre[:, width : width + tile], ((0, 0), (width, width), (0, 0)))
    value_mid = own - object_rate * grad_mid
    value_left = -object_rate * grad_left
    value_right = -object_rate * grad_right
    sent = jnp.concatenate([value_left, value_mid[:, :, :half]], axis=2)
    got = shifted(sent, "col", -1)
    wide = jnp.concatenate(
        [
            value_mid[:, :, half : tile - width],
            value_mid[:, :, tile - width :] + got[:, :, :width],
            value_right + got[:, :, width : 2 * width],
            got[:, :, 2 * width :],
        ],
        axis=2,
    )
    got = shifted(wide[:, : width + half], "row", -1)
    moved = jnp.concatenate(
        [
            wide[:, width + half : tile],
            wide[:, tile : tile + width] + got[:, :width],
            wide[:, tile + width :] + got[:, width : 2 * width],
            got[:, 2 * width :],
        ],
        axis=1,
    )
    return (moved, probe_now - probe_gain / frames_total * probe_total)


def solution(mesh):
    in_specs = (
        P(None, "row", "col"),
        P(),
        P(("row", "col"), None, None),
        P(("row", "col"), None),
        P(("row", "col")),
    )
    out_specs = (P(None, "row", "col"), P())
    return jax.shard_map(
        on_device, mesh=mesh, in_specs=in_specs, out_specs=out_specs, check_vma=False
    )
```

time: 1020 us -> 295 us (0.29); the launches traced: 1010 us -> 291 us
  waiting for transfers between devices: 454 us -> 79.7 us
  local copies, waits for them, and re-layouts: 313 us -> 17.1 us
  starting transfers between devices: 31.1 us -> 134 us
  loops' own time: 93.7 us -> 0 us
  other arithmetic: 82.9 us -> 17.4 us
  Pallas kernels: 0 us -> 42 us
  matrix products: 15.2 us -> 0 us
  between operations: 14.9 us -> 1.07 us
    psum x2 -> x0, waiting for transfers between devices: 305 us -> none  [iterate(): probe_total = lax.psum(probe_part, ('row', 'col'))]
    dynamic_update_slice x24 -> x6, local copies, waits for them, and re-layouts: 159 us -> 0.05 us  [probe_sum(): half = lax.dynamic_update_index_in_dim(half, value, (y - by) % y_count, 0)]
    ppermute x18 -> x44, starting transfers between devices: 31.1 us -> 134 us  [the longest x28 102 us: moved(): return lax.ppermute(array, ('row', 'col'), pairs)]
    gather x72 -> x0, local copies, waits for them, and re-layouts: 97.7 us -> none
    another operation x4 -> x0, loops' own time: 93.7 us -> none  [the longest x2 93.6 us: iterate(): lax.fori_loop(0, slot_count, add_slot, jnp.zeros(padded.shape, jnp.float32))]
    ppermute x18 -> x44, waiting for transfers between devices: 149 us -> 79.7 us  [the longest x28 46.2 us: moved(): return lax.ppermute(array, ('row', 'col'), pairs)]
    pallas_call x0 -> x2, Pallas kernels: none -> 42 us  [frames(): pl.pallas_call(kernel, out_shape=out_shapes, in_specs=[smem] + [vmem] * (...]
    add x26 -> x9, other arithmetic: 40.4 us -> 5.09 us  [the longest x1 2.17 us: on_device(): inner = grad_mid[:, :, width:tile - width] + add_inner]
  transfers between devices with their start and end apart: 20 -> 44, of which waited for: 16 -> 23; matrix products, arithmetic and copies ran while one was open for 1% -> 7% of each run, Pallas kernels for 0% -> 0%
where the time goes in v1:
time: 295 us; the launch traced here: 291 us
  starting transfers between devices  134 us (45%)
  waiting for transfers between devices  79.7 us (27%)
  Pallas kernels  42 us (14%)
  other arithmetic  17.4 us (6%)
  local copies, waits for them, and re-layouts  17.1 us (6%)
    ppermute x28, starting transfers between devices, moved(): return lax.ppermute(array, ('row', 'col'), pairs)  102 us
    ppermute x28, waiting for transfers between devices, moved(): return lax.ppermute(array, ('row', 'col'), pairs)  46.2 us
    pallas_call x2, Pallas kernels, frames(): pl.pallas_call(kernel, out_shape=out_shapes, in_specs=[smem] + [vmem] * (...  42 us
    ppermute x16, waiting for transfers between devices, shifted(): lax.ppermute(array, axis, [(i, (i + by) % count) for i in range(count)])  33.5 us
    ppermute x16, starting transfers between devices, shifted(): lax.ppermute(array, axis, [(i, (i + by) % count) for i in range(count)])  31.7 us
  transfers between devices with their start and end apart: 44, of which 23 were waited for; matrix products, arithmetic and copies ran while one was open for 7% of the time, Pallas kernels for 0%

profile of v1, /device:TPU:1, one launch (start us, length us, event | category | flops | bytes accessed | tf_op | source)
XLA Modules:
  0.0 291.0 jit_solution(11019504824570889295)
XLA Ops:
  0.6 2.2 fusion.17
  2.9 2.5 collective-permute-start
  5.4 2.2 collective-permute-start.1
  8.6 2.2 collective-permute-start.3
  10.8 22.0 %collective-permute-done = f32[2,128,512]{2,1,0:T(8,128)} collective-permute-done((f32[2,128,512]{2,1,0:T(8,128)S(1)}, f32[2,128,512]{2,1,0:T(8,128)}, u32[]{:S(2)}, u32[]{:S(2)}) %collective-permute-start) | collective-permute-done | bytes 524320 | tf_op jit(solution)/shard_map/ppermute | solution.py:157
  46.8 21.0 %frames.2 = (f32[2,768,128]{2,1,0:T(8,128)}, f32[2,768,512]{2,1,0:T(8,128)}, f32[2,768,128]{2,1,0:T(8,128)}, f32[2,256,256]{2,1,0:T(8,128)}) custom-call(s32[12,3]{1,0:T(8,128)} %copy.12.refs_0_, f32[2,768,128]{2,1,0:T(8,128)} %pad_maximum_fusion.3.refs_1_, f32[2,768,512]{2,1,0:T(8,128)} %copy-done.1, f32[2,768,128]{2,1,0:T(8,128)} %pad_maximum_fusion.4.refs_3_, ...), custom_call_target="tpu_custom_call" | custom-call | tf_op jit(solution)/shard_map/frames/pallas_call | solution.py:139
  68.7 9.8 %collective-permute-start.14 = (f32[256,256]{1,0:T(8,128)S(1)}, f32[256,256]{1,0:T(8,128)S(1)}, u32[]{:S(2)}, u32[]{:S(2)}) collective-permute-start(f32[256,256]{1,0:T(8,128)S(1)} %dynamic-slice_bitcast_fusion.1), channel_id=1, source_target_pairs={{0,1},{1,0},{2,3},{3,2},{4,5},{5,4},{6,7},{7,6},{16,17},{17,16},{1... | collective-permute-start | bytes 786440 | tf_op jit(solution)/shard_map/ppermute | solution.py:179
  80.7 3.0 %collective-permute-start.17 = (f32[64,256]{1,0:T(8,128)S(1)}, f32[64,256]{1,0:T(8,128)S(1)}, u32[]{:S(2)}, u32[]{:S(2)}) collective-permute-start(f32[64,256]{1,0:T(8,128)S(1)} %get-tuple-element.57), channel_id=1, source_target_pairs={{0,6},{1,7},{2,0},{3,1},{4,2},{5,3},{6,4},{7,5},{16,22},{17,23},{1... | collective-permute-start | bytes 196616 | tf_op jit(solution)/shard_map/ppermute | solution.py:179
  84.5 2.8 collective-permute-start.6
  90.0 2.5 collective-permute-start.20
  92.5 2.3 collective-permute-start.19
  94.8 2.3 fusion.15
  97.1 4.1 %collective-permute-start.11 = (f32[2,256,256]{2,1,0:T(8,128)}, f32[2,256,256]{2,1,0:T(8,128)}, u32[]{:S(2)}, u32[]{:S(2)}) collective-permute-start(f32[2,256,256]{2,1,0:T(8,128)} %get-tuple-element.29), channel_id=1, source_target_pairs={{0,112},{16,0},{32,16},{48,32},{64,48},{80,64},{96,80},{112,96},{1... | collective-permute-start | bytes 1572872 | tf_op jit(solution)/shard_map/ppermute | solution.py:157
  106.3 21.4 %collective-permute-done.23 = f32[64,256]{1,0:T(8,128)S(1)} collective-permute-done((f32[64,256]{1,0:T(8,128)S(1)}, f32[64,256]{1,0:T(8,128)S(1)}, u32[]{:S(2)}, u32[]{:S(2)}) %collective-permute-start.23) | collective-permute-done | bytes 65568 | tf_op jit(solution)/shard_map/ppermute | solution.py:179
  127.7 2.6 collective-permute-start.8
  130.4 6.6 %collective-permute-start.24 = (f32[64,256]{1,0:T(8,128)S(1)}, f32[64,256]{1,0:T(8,128)S(1)}, u32[]{:S(2)}, u32[]{:S(2)}) collective-permute-start(f32[64,256]{1,0:T(8,128)S(1)} %get-tuple-element.21), channel_id=1, source_target_pairs={{0,2},{1,3},{2,4},{3,5},{4,6},{5,7},{6,0},{7,1},{16,18},{17,19},{1... | collective-permute-start | bytes 196616 | tf_op jit(solution)/shard_map/ppermute | solution.py:179
  138.4 2.2 collective-permute-start.25
  140.6 2.8 collective-permute-done.25
  144.9 6.9 %collective-permute-done.9 = f32[2,256,256]{2,1,0:T(8,128)S(1)} collective-permute-done((f32[2,256,256]{2,1,0:T(8,128)S(1)}, f32[2,256,256]{2,1,0:T(8,128)S(1)}, u32[]{:S(2)}, u32[]{:S(2)}) %collective-permute-start.9) | collective-permute-done | bytes 524320 | tf_op jit(solution)/shard_map/ppermute | solution.py:157
  151.7 2.2 maximum_add_fusion
  159.2 5.4 %collective-permute-start.27 = (f32[256,256]{1,0:T(8,128)S(1)}, f32[256,256]{1,0:T(8,128)}, u32[]{:S(2)}, u32[]{:S(2)}) collective-permute-start(f32[256,256]{1,0:T(8,128)S(1)} %bitcast.66), channel_id=1, source_target_pairs={{0,1},{1,0},{2,3},{3,2},{4,5},{5,4},{6,7},{7,6},{16,17},{17,16},{1... | collective-permute-start | bytes 786440 | tf_op jit(solution)/shard_map/ppermute | solution.py:179
  169.9 21.0 %frames.3 = (f32[2,768,128]{2,1,0:T(8,128)}, f32[2,768,512]{2,1,0:T(8,128)}, f32[2,768,128]{2,1,0:T(8,128)}, f32[2,256,256]{2,1,0:T(8,128)}) custom-call(s32[12,3]{1,0:T(8,128)} %copy.12.refs_0_, f32[2,768,128]{2,1,0:T(8,128)} %collective-permute-done.12.refs_1_, f32[2,768,512]{2,1,0:T(8,128)} %copy-done, f32[2,768,128]{2,1,0:T(8,128)} %collective-permute-done.13.refs_3_, ...), custom_call_target="tpu_custom_call" | custom-call | tf_op jit(solution)/shard_map/frames/pallas_call | solution.py:139
  190.8 2.7 multiply_subtract_fusion
  194.9 8.3 %collective-permute-start.28 = (f32[2,768,384]{2,1,0:T(8,128)S(1)}, f32[2,768,384]{2,1,0:T(8,128)S(1)}, u32[]{:S(2)}, u32[]{:S(2)}) collective-permute-start(f32[2,768,384]{2,1,0:T(8,128)S(1)} %pad_maximum_fusion.1), channel_id=1, source_target_pairs={{0,15},{1,0},{2,1},{3,2},{4,3},{5,4},{6,5},{7,6},{8,7},{9,8},{10,9... | collective-permute-start | bytes 7077896 | tf_op jit(solution)/shard_map/ppermute | solution.py:157
  204.1 3.6 %collective-permute-done.30 = f32[256,256]{1,0:T(8,128)S(1)} collective-permute-done((f32[256,256]{1,0:T(8,128)S(1)}, f32[256,256]{1,0:T(8,128)S(1)}, u32[]{:S(2)}, u32[]{:S(2)}) %collective-permute-start.30) | collective-permute-done | bytes 262176 | tf_op jit(solution)/shard_map/ppermute | solution.py:179
  207.9 2.8 collective-permute-start.33
  210.6 2.7 collective-permute-start.32
  215.2 2.5 collective-permute-done.31
  223.3 4.9 %collective-permute-start.39 = (f32[64,256]{1,0:T(8,128)S(1)}, f32[64,256]{1,0:T(8,128)S(1)}, u32[]{:S(2)}, u32[]{:S(2)}) collective-permute-start(f32[64,256]{1,0:T(8,128)S(1)} %add_add_fusion.1), channel_id=1, source_target_pairs={{0,24},{1,25},{2,26},{3,27},{4,28},{5,29},{6,30},{7,31},{16,0},{17... | collective-permute-start | bytes 196616 | tf_op jit(solution)/shard_map/ppermute | solution.py:179
  229.6 4.1 %collective-permute-start.29 = (f32[2,384,512]{2,1,0:T(8,128)S(1)}, f32[2,384,512]{2,1,0:T(8,128)S(1)}, u32[]{:S(2)}, u32[]{:S(2)}) collective-permute-start(f32[2,384,512]{2,1,0:T(8,128)S(1)} %slice.169), channel_id=1, source_target_pairs={{0,112},{16,0},{32,16},{48,32},{64,48},{80,64},{96,80},{112,96},{1... | collective-permute-start | bytes 4718600 | tf_op jit(solution)/shard_map/ppermute | solution.py:157
  233.8 9.9 %collective-permute-start.41 = (f32[64,256]{1,0:T(8,128)S(1)}, f32[64,256]{1,0:T(8,128)S(1)}, u32[]{:S(2)}, u32[]{:S(2)}) collective-permute-start(f32[64,256]{1,0:T(8,128)S(1)} %get-tuple-element.19), channel_id=1, source_target_pairs={{0,4},{1,5},{2,6},{3,7},{4,0},{5,1},{6,2},{7,3},{16,20},{17,21},{1... | collective-permute-start | bytes 196616 | tf_op jit(solution)/shard_map/ppermute | solution.py:179
  246.9 40.2 %collective-permute-start.43 = (f32[256,256]{1,0:T(8,128)S(1)}, f32[256,256]{1,0:T(8,128)S(1)}, u32[]{:S(2)}, u32[]{:S(2)}) collective-permute-start(f32[256,256]{1,0:T(8,128)S(1)} %bitcast.65), channel_id=1, source_target_pairs={{0,1},{1,0},{2,3},{3,2},{4,5},{5,4},{6,7},{7,6},{16,17},{17,16},{1... | collective-permute-start | bytes 786440 | tf_op jit(solution)/shard_map/ppermute | solution.py:179
  (139 shorter events, 58.3 us)
Async XLA Ops:
  2.9 29.9 %collective-permute-start = (f32[2,128,512]{2,1,0:T(8,128)S(1)}, f32[2,128,512]{2,1,0:T(8,128)}, u32[]{:S(2)}, u32[]{:S(2)}) collective-permute-start(f32[2,128,512]{2,1,0:T(8,128)S(1)} %get-tuple-element.37), channel_id=1, source_target_pairs={{0,16},{16,32},{32,48},{48,64},{64,80},{80,96},{96,112},{112,0},{1... | collective-permute-start | bytes 1572872 | tf_op jit(solution)/shard_map/ppermute | solution.py:157
  5.4 30.4 %collective-permute-start.1 = (f32[2,128,512]{2,1,0:T(8,128)}, f32[2,128,512]{2,1,0:T(8,128)}, u32[]{:S(2)}, u32[]{:S(2)}) collective-permute-start(f32[2,128,512]{2,1,0:T(8,128)} %get-tuple-element.36), channel_id=1, source_target_pairs={{0,112},{16,0},{32,16},{48,32},{64,48},{80,64},{96,80},{112,96},{1... | collective-permute-start | bytes 1572872 | tf_op jit(solution)/shard_map/ppermute | solution.py:157
  8.6 32.9 %collective-permute-start.3 = (f32[2,512,128]{2,1,0:T(8,128)}, f32[2,512,128]{2,1,0:T(8,128)}, u32[]{:S(2)}, u32[]{:S(2)}) collective-permute-start(f32[2,512,128]{2,1,0:T(8,128)} %get-tuple-element.35), channel_id=1, source_target_pairs={{0,1},{1,2},{2,3},{3,4},{4,5},{5,6},{6,7},{7,8},{8,9},{9,10},{10,1... | collective-permute-start | bytes 1572872 | tf_op jit(solution)/shard_map/ppermute | solution.py:157
  10.7 34.0 %collective-permute-start.5 = (f32[2,512,128]{2,1,0:T(8,128)}, f32[2,512,128]{2,1,0:T(8,128)}, u32[]{:S(2)}, u32[]{:S(2)}) collective-permute-start(f32[2,512,128]{2,1,0:T(8,128)} %get-tuple-element.34), channel_id=1, source_target_pairs={{0,15},{1,0},{2,1},{3,2},{4,3},{5,4},{6,5},{7,6},{8,7},{9,8},{10,9... | collective-permute-start | bytes 1572872 | tf_op jit(solution)/shard_map/ppermute | solution.py:157
  38.7 6.0 %collective-permute-start.4 = (f32[2,256,128]{2,1,0:T(8,128)}, f32[2,256,128]{2,1,0:T(8,128)S(1)}, u32[]{:S(2)}, u32[]{:S(2)}) collective-permute-start(f32[2,256,128]{2,1,0:T(8,128)} %get-tuple-element.43), channel_id=1, source_target_pairs={{0,15},{1,0},{2,1},{3,2},{4,3},{5,4},{6,5},{7,6},{8,7},{9,8},{10,9... | collective-permute-start | bytes 786440 | tf_op jit(solution)/shard_map/ppermute | solution.py:157
  68.7 11.0 %collective-permute-start.14 = (f32[256,256]{1,0:T(8,128)S(1)}, f32[256,256]{1,0:T(8,128)S(1)}, u32[]{:S(2)}, u32[]{:S(2)}) collective-permute-start(f32[256,256]{1,0:T(8,128)S(1)} %dynamic-slice_bitcast_fusion.1), channel_id=1, source_target_pairs={{0,1},{1,0},{2,3},{3,2},{4,5},{5,4},{6,7},{7,6},{16,17},{17,16},{1... | collective-permute-start | bytes 786440 | tf_op jit(solution)/shard_map/ppermute | solution.py:179
  80.7 6.5 %collective-permute-start.17 = (f32[64,256]{1,0:T(8,128)S(1)}, f32[64,256]{1,0:T(8,128)S(1)}, u32[]{:S(2)}, u32[]{:S(2)}) collective-permute-start(f32[64,256]{1,0:T(8,128)S(1)} %get-tuple-element.57), channel_id=1, source_target_pairs={{0,6},{1,7},{2,0},{3,1},{4,2},{5,3},{6,4},{7,5},{16,22},{17,23},{1... | collective-permute-start | bytes 196616 | tf_op jit(solution)/shard_map/ppermute | solution.py:179
  83.7 6.2 %collective-permute-start.15 = (f32[64,256]{1,0:T(8,128)S(1)}, f32[64,256]{1,0:T(8,128)S(1)}, u32[]{:S(2)}, u32[]{:S(2)}) collective-permute-start(f32[64,256]{1,0:T(8,128)S(1)} %get-tuple-element.56), channel_id=1, source_target_pairs={{0,2},{1,3},{2,4},{3,5},{4,6},{5,7},{6,0},{7,1},{16,18},{17,19},{1... | collective-permute-start | bytes 196616 | tf_op jit(solution)/shard_map/ppermute | solution.py:179
  84.5 18.4 %collective-permute-start.6 = (f32[2,768,128]{2,1,0:T(8,128)}, f32[2,768,128]{2,1,0:T(8,128)S(1)}, u32[]{:S(2)}, u32[]{:S(2)}) collective-permute-start(f32[2,768,128]{2,1,0:T(8,128)} %get-tuple-element.11), channel_id=1, source_target_pairs={{0,1},{1,2},{2,3},{3,4},{4,5},{5,6},{6,7},{7,8},{8,9},{9,10},{10,1... | collective-permute-start | bytes 2359304 | tf_op jit(solution)/shard_map/ppermute | solution.py:157
  87.3 16.6 %collective-permute-start.7 = (f32[2,768,128]{2,1,0:T(8,128)}, f32[2,768,128]{2,1,0:T(8,128)S(1)}, u32[]{:S(2)}, u32[]{:S(2)}) collective-permute-start(f32[2,768,128]{2,1,0:T(8,128)} %get-tuple-element.12), channel_id=1, source_target_pairs={{0,15},{1,0},{2,1},{3,2},{4,3},{5,4},{6,5},{7,6},{8,7},{9,8},{10,9... | collective-permute-start | bytes 2359304 | tf_op jit(solution)/shard_map/ppermute | solution.py:157
  90.0 7.1 %collective-permute-start.20 = (f32[64,256]{1,0:T(8,128)S(1)}, f32[64,256]{1,0:T(8,128)S(1)}, u32[]{:S(2)}, u32[]{:S(2)}) collective-permute-start(f32[64,256]{1,0:T(8,128)S(1)} %fusion.10), channel_id=1, source_target_pairs={{0,96},{1,97},{2,98},{3,99},{4,100},{5,101},{6,102},{7,103},{16,11... | collective-permute-start | bytes 196616 | tf_op jit(solution)/shard_map/ppermute | solution.py:179
  92.5 8.6 %collective-permute-start.19 = (f32[64,256]{1,0:T(8,128)S(1)}, f32[64,256]{1,0:T(8,128)S(1)}, u32[]{:S(2)}, u32[]{:S(2)}) collective-permute-start(f32[64,256]{1,0:T(8,128)S(1)} %fusion.10), channel_id=1, source_target_pairs={{0,64},{1,65},{2,66},{3,67},{4,68},{5,69},{6,70},{7,71},{16,80},{1... | collective-permute-start | bytes 196616 | tf_op jit(solution)/shard_map/ppermute | solution.py:179
  94.8 6.3 %collective-permute-start.18 = (f32[64,256]{1,0:T(8,128)S(1)}, f32[64,256]{1,0:T(8,128)S(1)}, u32[]{:S(2)}, u32[]{:S(2)}) collective-permute-start(f32[64,256]{1,0:T(8,128)S(1)} %fusion.10), channel_id=1, source_target_pairs={{0,32},{1,33},{2,34},{3,35},{4,36},{5,37},{6,38},{7,39},{16,48},{1... | collective-permute-start | bytes 196616 | tf_op jit(solution)/shard_map/ppermute | solution.py:179
  97.1 47.8 %collective-permute-start.11 = (f32[2,256,256]{2,1,0:T(8,128)}, f32[2,256,256]{2,1,0:T(8,128)}, u32[]{:S(2)}, u32[]{:S(2)}) collective-permute-start(f32[2,256,256]{2,1,0:T(8,128)} %get-tuple-element.29), channel_id=1, source_target_pairs={{0,112},{16,0},{32,16},{48,32},{64,48},{80,64},{96,80},{112,96},{1... | collective-permute-start | bytes 1572872 | tf_op jit(solution)/shard_map/ppermute | solution.py:157
  101.1 43.7 %collective-permute-start.10 = (f32[2,256,256]{2,1,0:T(8,128)}, f32[2,256,256]{2,1,0:T(8,128)}, u32[]{:S(2)}, u32[]{:S(2)}) collective-permute-start(f32[2,256,256]{2,1,0:T(8,128)} %get-tuple-element.28), channel_id=1, source_target_pairs={{0,16},{16,32},{32,48},{48,64},{64,80},{80,96},{96,112},{112,0},{1... | collective-permute-start | bytes 1572872 | tf_op jit(solution)/shard_map/ppermute | solution.py:157
  101.2 26.4 %collective-permute-start.23 = (f32[64,256]{1,0:T(8,128)S(1)}, f32[64,256]{1,0:T(8,128)S(1)}, u32[]{:S(2)}, u32[]{:S(2)}) collective-permute-start(f32[64,256]{1,0:T(8,128)S(1)} %add_add_fusion.3), channel_id=1, source_target_pairs={{0,24},{1,25},{2,26},{3,27},{4,28},{5,29},{6,30},{7,31},{16,0},{17... | collective-permute-start | bytes 196616 | tf_op jit(solution)/shard_map/ppermute | solution.py:179
  102.9 24.9 %collective-permute-start.22 = (f32[64,256]{1,0:T(8,128)S(1)}, f32[64,256]{1,0:T(8,128)S(1)}, u32[]{:S(2)}, u32[]{:S(2)}) collective-permute-start(f32[64,256]{1,0:T(8,128)S(1)} %add_add_fusion.3), channel_id=1, source_target_pairs={{0,8},{1,9},{2,10},{3,11},{4,12},{5,13},{6,14},{7,15},{16,24},{17,... | collective-permute-start | bytes 196616 | tf_op jit(solution)/shard_map/ppermute | solution.py:179
  103.9 26.5 %collective-permute-start.21 = (f32[64,256]{1,0:T(8,128)S(1)}, f32[64,256]{1,0:T(8,128)S(1)}, u32[]{:S(2)}, u32[]{:S(2)}) collective-permute-start(f32[64,256]{1,0:T(8,128)S(1)} %add_add_fusion.3), channel_id=1, source_target_pairs={{0,16},{1,17},{2,18},{3,19},{4,20},{5,21},{6,22},{7,23},{16,8},{17... | collective-permute-start | bytes 196616 | tf_op jit(solution)/shard_map/ppermute | solution.py:179
  127.6 24.1 %collective-permute-start.9 = (f32[2,256,256]{2,1,0:T(8,128)S(1)}, f32[2,256,256]{2,1,0:T(8,128)S(1)}, u32[]{:S(2)}, u32[]{:S(2)}) collective-permute-start(f32[2,256,256]{2,1,0:T(8,128)S(1)} %get-tuple-element.42), channel_id=1, source_target_pairs={{0,112},{16,0},{32,16},{48,32},{64,48},{80,64},{96,80},{112,96},{1... | collective-permute-start | bytes 1572872 | tf_op jit(solution)/shard_map/ppermute | solution.py:157
  127.7 24.0 %collective-permute-start.8 = (f32[2,256,256]{2,1,0:T(8,128)S(1)}, f32[2,256,256]{2,1,0:T(8,128)}, u32[]{:S(2)}, u32[]{:S(2)}) collective-permute-start(f32[2,256,256]{2,1,0:T(8,128)S(1)} %get-tuple-element.41), channel_id=1, source_target_pairs={{0,16},{16,32},{32,48},{48,64},{64,80},{80,96},{96,112},{112,0},{1... | collective-permute-start | bytes 1572872 | tf_op jit(solution)/shard_map/ppermute | solution.py:157
  130.4 8.0 %collective-permute-start.24 = (f32[64,256]{1,0:T(8,128)S(1)}, f32[64,256]{1,0:T(8,128)S(1)}, u32[]{:S(2)}, u32[]{:S(2)}) collective-permute-start(f32[64,256]{1,0:T(8,128)S(1)} %get-tuple-element.21), channel_id=1, source_target_pairs={{0,2},{1,3},{2,4},{3,5},{4,6},{5,7},{6,0},{7,1},{16,18},{17,19},{1... | collective-permute-start | bytes 196616 | tf_op jit(solution)/shard_map/ppermute | solution.py:179
  143.4 15.8 %collective-permute-start.26 = (f32[64,256]{1,0:T(8,128)S(1)}, f32[64,256]{1,0:T(8,128)S(1)}, u32[]{:S(2)}, u32[]{:S(2)}) collective-permute-start(f32[64,256]{1,0:T(8,128)S(1)} %get-tuple-element.21), channel_id=1, source_target_pairs={{0,6},{1,7},{2,0},{3,1},{4,2},{5,3},{6,4},{7,5},{16,22},{17,23},{1... | collective-permute-start | bytes 196616 | tf_op jit(solution)/shard_map/ppermute | solution.py:179
  157.8 10.1 %collective-permute-start.12 = (f32[2,768,128]{2,1,0:T(8,128)}, f32[2,768,128]{2,1,0:T(8,128)}, u32[]{:S(2)}, u32[]{:S(2)}) collective-permute-start(f32[2,768,128]{2,1,0:T(8,128)} %get-tuple-element.27), channel_id=1, source_target_pairs={{0,1},{1,2},{2,3},{3,4},{4,5},{5,6},{6,7},{7,8},{8,9},{9,10},{10,1... | collective-permute-start | bytes 2359304 | tf_op jit(solution)/shard_map/ppermute | solution.py:157
  157.8 12.0 %collective-permute-start.13 = (f32[2,768,128]{2,1,0:T(8,128)}, f32[2,768,128]{2,1,0:T(8,128)}, u32[]{:S(2)}, u32[]{:S(2)}) collective-permute-start(f32[2,768,128]{2,1,0:T(8,128)} %get-tuple-element.26), channel_id=1, source_target_pairs={{0,15},{1,0},{2,1},{3,2},{4,3},{5,4},{6,5},{7,6},{8,7},{9,8},{10,9... | collective-permute-start | bytes 2359304 | tf_op jit(solution)/shard_map/ppermute | solution.py:157
  159.2 6.7 %collective-permute-start.27 = (f32[256,256]{1,0:T(8,128)S(1)}, f32[256,256]{1,0:T(8,128)}, u32[]{:S(2)}, u32[]{:S(2)}) collective-permute-start(f32[256,256]{1,0:T(8,128)S(1)} %bitcast.66), channel_id=1, source_target_pairs={{0,1},{1,0},{2,3},{3,2},{4,5},{5,4},{6,7},{7,6},{16,17},{17,16},{1... | collective-permute-start | bytes 786440 | tf_op jit(solution)/shard_map/ppermute | solution.py:179
  194.9 34.0 %collective-permute-start.28 = (f32[2,768,384]{2,1,0:T(8,128)S(1)}, f32[2,768,384]{2,1,0:T(8,128)S(1)}, u32[]{:S(2)}, u32[]{:S(2)}) collective-permute-start(f32[2,768,384]{2,1,0:T(8,128)S(1)} %pad_maximum_fusion.1), channel_id=1, source_target_pairs={{0,15},{1,0},{2,1},{3,2},{4,3},{5,4},{6,5},{7,6},{8,7},{9,8},{10,9... | collective-permute-start | bytes 7077896 | tf_op jit(solution)/shard_map/ppermute | solution.py:157
  207.9 6.2 %collective-permute-start.33 = (f32[64,256]{1,0:T(8,128)S(1)}, f32[64,256]{1,0:T(8,128)S(1)}, u32[]{:S(2)}, u32[]{:S(2)}) collective-permute-start(f32[64,256]{1,0:T(8,128)S(1)} %get-tuple-element.54), channel_id=1, source_target_pairs={{0,6},{1,7},{2,0},{3,1},{4,2},{5,3},{6,4},{7,5},{16,22},{17,23},{1... | collective-permute-start | bytes 196616 | tf_op jit(solution)/shard_map/ppermute | solution.py:179
  223.3 10.3 %collective-permute-start.39 = (f32[64,256]{1,0:T(8,128)S(1)}, f32[64,256]{1,0:T(8,128)S(1)}, u32[]{:S(2)}, u32[]{:S(2)}) collective-permute-start(f32[64,256]{1,0:T(8,128)S(1)} %add_add_fusion.1), channel_id=1, source_target_pairs={{0,24},{1,25},{2,26},{3,27},{4,28},{5,29},{6,30},{7,31},{16,0},{17... | collective-permute-start | bytes 196616 | tf_op jit(solution)/shard_map/ppermute | solution.py:179
  229.6 59.6 %collective-permute-start.29 = (f32[2,384,512]{2,1,0:T(8,128)S(1)}, f32[2,384,512]{2,1,0:T(8,128)S(1)}, u32[]{:S(2)}, u32[]{:S(2)}) collective-permute-start(f32[2,384,512]{2,1,0:T(8,128)S(1)} %slice.169), channel_id=1, source_target_pairs={{0,112},{16,0},{32,16},{48,32},{64,48},{80,64},{96,80},{112,96},{1... | collective-permute-start | bytes 4718600 | tf_op jit(solution)/shard_map/ppermute | solution.py:157
  233.7 10.5 %collective-permute-start.40 = (f32[64,256]{1,0:T(8,128)S(1)}, f32[64,256]{1,0:T(8,128)S(1)}, u32[]{:S(2)}, u32[]{:S(2)}) collective-permute-start(f32[64,256]{1,0:T(8,128)S(1)} %get-tuple-element.19), channel_id=1, source_target_pairs={{0,2},{1,3},{2,4},{3,5},{4,6},{5,7},{6,0},{7,1},{16,18},{17,19},{1... | collective-permute-start | bytes 196616 | tf_op jit(solution)/shard_map/ppermute | solution.py:179
  233.8 12.3 %collective-permute-start.41 = (f32[64,256]{1,0:T(8,128)S(1)}, f32[64,256]{1,0:T(8,128)S(1)}, u32[]{:S(2)}, u32[]{:S(2)}) collective-permute-start(f32[64,256]{1,0:T(8,128)S(1)} %get-tuple-element.19), channel_id=1, source_target_pairs={{0,4},{1,5},{2,6},{3,7},{4,0},{5,1},{6,2},{7,3},{16,20},{17,21},{1... | collective-permute-start | bytes 196616 | tf_op jit(solution)/shard_map/ppermute | solution.py:179
  246.9 41.4 %collective-permute-start.43 = (f32[256,256]{1,0:T(8,128)S(1)}, f32[256,256]{1,0:T(8,128)S(1)}, u32[]{:S(2)}, u32[]{:S(2)}) collective-permute-start(f32[256,256]{1,0:T(8,128)S(1)} %bitcast.65), channel_id=1, source_target_pairs={{0,1},{1,0},{2,3},{3,2},{4,5},{5,4},{6,7},{7,6},{16,17},{17,16},{1... | collective-permute-start | bytes 786440 | tf_op jit(solution)/shard_map/ppermute | solution.py:179
  (24 other events, 215.4 us)
